TPU v7x, 256 devices: a whole 4x4x8 slice. The times are simulated.
256 devices in a mesh: grp: 64 (over z, y, core), tp: 4 (over x).
Axes of the slice: x: 4, y: 4, z: 8, core: 2. Of those that a mesh axis runs over, the one named last changes fastest.
Arguments:
- roll_query: bfloat16 [16384, 5120], P(('grp', 'tp')), may hold values from -6 to 6
- roll_key: bfloat16 [16384, 1024], P(('grp', 'tp')), may hold values from -6 to 6
- roll_value: bfloat16 [16384, 1024], P(('grp', 'tp')), may hold values from -6 to 6
- roll_cotangent: bfloat16 [16384, 5120], P(('grp', 'tp')), may hold values from -6 to 6
- route: int32 [16384], P(('grp', 'tp')), may hold values from 0 to 127, as said below
- arrival: int32 [16384], P('grp'), may hold values from 0 to 511, as said below
- lengths: int32 [64, 4], P('grp'), may hold values from 1 to 128, 256 in all within a row
- prefix_kv: bfloat16 [64, 512, 2, 1024], P('grp', None, None, 'tp'), may hold values from -6 to 6
- owner: int32 [16], replicated, may hold values from 0 to 3
Outputs:
- grad_query: bfloat16 [16384, 5120], P(('grp', 'tp'))
- grad_key: bfloat16 [16384, 1024], P(('grp', 'tp'))
- grad_value: bfloat16 [16384, 1024], P(('grp', 'tp'))
- grad_prefix: float32 [64, 512, 2, 1024], P('grp', None, None, 'tp')
Inputs may be any that keep to these rules, and one draw needn't show every extreme that they name: `route`: each entry is t * 2 + s: the token goes to trainer t (a grp index) into slot s. The tokens of one rollout device sent to one trainer take slots 0, 1, ... without gaps, at most 2 of them; every device sends exactly 2 to some trainer, every trainer receives exactly 256 tokens and exactly 2 from some device. `arrival`: entry t * 256 + j is r * 8 + p * 2 + s for the token that the rollout device with grp index r and tp index p sends to trainer t into slot s; the 256 entries of a trainer name each token sent to it once.
All inputs are finite; a program needn't handle non-finite values.
Results may differ from a plain program's by a relative error of at most 0.0073.
Values may be sent and summed in bfloat16 or wider, within the bound.
A program may use at most 64 MiB of HBM per device.

v0:
```python
import functools
import math

import jax
import jax.numpy as jnp
from jax import lax
from jax.experimental import pallas as pl
from jax.experimental.pallas import tpu as pltpu
from jax.sharding import PartitionSpec as P

MESH = pl.DeviceIdType.MESH
D = 128
TP = 4
PLANE = 8
RATIO = 5
KH = 2
ROWS = 256
SEND = 64
PRE = 512
CHUNKS = 6
WIDE = 512
BACKS = 8
BACK = 256
PITCH = 128
NEGATIVE = -1e30
SCALE = 1.0 / math.sqrt(D)
F32 = jnp.float32
BF16 = jnp.bfloat16
I32 = jnp.int32
WIDTHS = (128, 256, 256, 256)


def iota(shape, dim):
    return lax.broadcasted_iota(I32, shape, dim)


def hot(match):
    return jnp.where(match, 1.0, 0.0).astype(BF16)


def dot(a, b):
    return jnp.dot(a, b, preferred_element_type=F32)


def dot_nt(a, b):
    return lax.dot_general(a, b, (((1,), (1,)), ((), ())), preferred_element_type=F32)


def place(kind, valid, lanes, limit):
    classes = iota((8, lanes), 0)
    member = (kind == classes) & valid
    before = hot(iota((lanes, lanes), 0) < iota((lanes, lanes), 1))
    count = dot(hot(member), before)
    rank = jnp.sum(jnp.where(member, count, 0.0), axis=0, keepdims=True).astype(I32)
    kind, valid = kind[0:1], valid[0:1]
    slot = jnp.where(valid & (rank < limit), kind * limit + rank, -1)
    table = jnp.where(valid & (rank < limit), kind * PITCH + rank, -1)
    return slot, table


def tabulate(code, table, lanes):
    sub = iota((8, lanes), 0)
    high, low = code >> 7, code & 127
    parts = jnp.where(sub == 0, high, jnp.where(sub == 1, low, 0)).astype(F32).astype(BF16)
    spread = hot(iota((8 * PITCH, lanes), 0) == table)
    return dot_nt(parts, spread)


def compacted(table, limit):
    lanes = 8 * limit
    lane = iota((8 * PITCH, lanes), 1)
    target = lane
    for i in range(1, 8):
        target = target + jnp.where(lane >= i * limit, PITCH - limit, 0)
    pick = hot(iota((8 * PITCH, lanes), 0) == target)
    parts = dot(table.astype(BF16), pick)
    return (parts[0:1] * 128.0 + parts[1:2]).astype(I32)


def turned(matrix):
    n = matrix.shape[1]
    eye = hot(iota((n, n), 0) == iota((n, n), 1))
    return dot_nt(eye, matrix).astype(BF16)


def kernel(
    cap_y,
    cap_z,
    query,
    key,
    value,
    cotangent,
    route,
    arrival,
    lengths,
    prefix,
    holder,
    grad_query,
    grad_key,
    grad_value,
    grad_prefix,
    x_table,
    y_table_out,
    y_table_in,
    z_table_out,
    z_table_in,
    x_in,
    y_out,
    y_in,
    z_out,
    z_in,
    bz_out,
    bz_in,
    by_out,
    by_in,
    bx_out,
    pre_in,
    pre_now,
    pre_far,
    to_y,
    to_z,
    to_rows,
    from_y,
    from_z,
    from_rows,
    mask,
    acc,
    acc_in,
    chip,
    chip_in,
    total,
    t_send,
    t_recv,
    x_send,
    x_recv,
    y_send,
    y_recv,
    z_send,
    z_recv,
    bz_send,
    bz_recv,
    by_send,
    by_recv,
    bx_send,
    bx_recv,
    p_send,
    p_recv,
    a_send,
    a_recv,
):
    grp = lax.axis_index("grp")
    tp = lax.axis_index("tp")
    plane = grp // PLANE
    spot = lax.rem(grp, PLANE)
    core = lax.rem(spot, 2)
    side = lax.rem(spot // 2, 2)
    mate = grp + 1 - 2 * core
    across = grp + 2 - 4 * side

    def x_peer(k):
        return lax.rem(tp + k, TP)

    def y_peer(k):
        return lax.rem(spot + k, PLANE)

    def z_peer(k):
        return lax.rem(plane + k, PLANE)

    def at_x(k):
        return (grp, x_peer(k))

    def at_y(k):
        return (plane * PLANE + y_peer(k), tp)

    def at_z(k):
        return (z_peer(k) * PLANE + spot, tp)

    def block(index, size):
        return pl.ds(pl.multiple_of(index * size, size), size)

    def remote(src, dst, send, recv, device):
        copy = pltpu.make_async_remote_copy(
            src_ref=src,
            dst_ref=dst,
            send_sem=send,
            recv_sem=recv,
            device_id=device,
            device_id_type=MESH,
        )
        copy.start()
        return copy

    def local(src, dst, sem):
        pltpu.make_async_copy(src, dst, sem).start()

    def await_bytes(ref, sem):
        pltpu.make_async_copy(ref, ref, sem).wait()

    entry = pltpu.get_barrier_semaphore()
    for k in range(1, TP):
        pl.semaphore_signal(entry, inc=1, device_id=at_x(k), device_id_type=MESH)
    for k in range(1, PLANE):
        pl.semaphore_signal(entry, inc=1, device_id=at_y(k), device_id_type=MESH)
    for k in range(1, PLANE):
        pl.semaphore_signal(entry, inc=1, device_id=at_z(k), device_id_type=MESH)
    pl.semaphore_wait(entry, TP - 1 + 2 * (PLANE - 1))

    for k in range(1, TP):
        remote(route, x_table.at[k - 1], t_send.at[0], t_recv.at[0], at_x(k))

    def chunk_parts(chunk, to):
        kh, part = chunk // 3, chunk % 3
        head = to * (KH * RATIO) + kh * RATIO
        if part == 0:
            return (
                (key, to * KH + kh, 1),
                (value, to * KH + kh, 1),
                (query, head, 1),
                (cotangent, head, 1),
            )
        first = head + 2 * part - 1
        return ((query, first, 2), (cotangent, first, 2))

    def x_stage(chunk):
        for k in range(TP):
            to = x_peer(k)
            lane = 0
            for source, head, heads in chunk_parts(chunk, to):
                src = source.at[:, pl.ds(pl.multiple_of(head * D, D), heads * D)]
                dst = x_in.at[chunk, block(tp, SEND), pl.ds(lane, heads * D)]
                if k == 0:
                    local(src, dst, x_recv.at[chunk])
                else:
                    remote(src, dst, x_send.at[chunk], x_recv.at[chunk], at_x(k))
                lane += heads * D

    x_stage(0)
    remote(prefix, pre_in, p_send.at[0], p_recv.at[0], (mate, tp))
    for chunk in range(1, CHUNKS):
        x_stage(chunk)

    await_bytes(x_table, t_recv.at[0])
    routes = route[...] + x_table[0] + x_table[1] + x_table[2]
    trainer = routes >> 1
    line = iota((8, ROWS), 1) // SEND
    number = grp * (2 * TP) + line * 2 + (routes & 1)
    code = ((trainer >> 3) * 512 + number + 1)[0:1]
    slot, table = place(trainer & 7, trainer >= 0, ROWS, cap_y)
    to_y[...] = hot(iota((8 * cap_y, ROWS), 0) == slot)
    y_table_out[...] = tabulate(code, table, ROWS)
    for k in range(1, PLANE):
        remote(
            y_table_out.at[:, block(y_peer(k), PITCH)],
            y_table_in.at[:, block(spot, PITCH)],
            t_send.at[1],
            t_recv.at[1],
            at_y(k),
        )
    local(
        y_table_out.at[:, block(spot, PITCH)], y_table_in.at[:, block(spot, PITCH)], t_recv.at[1]
    )

    def y_stage(chunk):
        await_bytes(x_in.at[chunk], x_recv.at[chunk])
        y_out[chunk] = dot(to_y[...], x_in[chunk]).astype(BF16)
        for k in range(1, PLANE):
            remote(
                y_out.at[chunk, block(y_peer(k), cap_y)],
                y_in.at[chunk, block(spot, cap_y)],
                y_send.at[chunk],
                y_recv.at[chunk],
                at_y(k),
            )
        local(
            y_out.at[chunk, block(spot, cap_y)],
            y_in.at[chunk, block(spot, cap_y)],
            y_recv.at[chunk],
        )

    def z_stage(chunk):
        await_bytes(y_in.at[chunk], y_recv.at[chunk])
        z_out[chunk] = dot(to_z[...], y_in[chunk]).astype(BF16)
        for k in (4, 3, 5, 2, 6, 1, 7):
            remote(
                z_out.at[chunk, block(z_peer(k), cap_z)],
                z_in.at[chunk, block(plane, cap_z)],
                z_send.at[chunk],
                z_recv.at[chunk],
                at_z(k),
            )
        local(
            z_out.at[chunk, block(plane, cap_z)],
            z_in.at[chunk, block(plane, cap_z)],
            z_recv.at[chunk],
        )

    y_stage(0)
    y_stage(1)

    await_bytes(y_table_in, t_recv.at[1])
    code = compacted(y_table_in[...], cap_y)
    lanes = 8 * cap_y
    code8 = jnp.broadcast_to(code, (8, lanes))
    slot, table = place((code8 - 1) >> 9, code8 > 0, lanes, cap_z)
    to_z[...] = hot(iota((8 * cap_z, lanes), 0) == slot)
    z_table_out[...] = tabulate(((code - 1) & 511) + 1, table, lanes)
    for k in range(1, PLANE):
        remote(
            z_table_out.at[:, block(z_peer(k), PITCH)],
            z_table_in.at[:, block(plane, PITCH)],
            t_send.at[2],
            t_recv.at[2],
            at_z(k),
        )
    local(
        z_table_out.at[:, block(plane, PITCH)], z_table_in.at[:, block(plane, PITCH)], t_recv.at[2]
    )

    z_stage(0)

    hold = holder[0:1, :]
    await_bytes(pre_in, p_recv.at[0])
    mine = (hold & 1) == core
    pre_now[...] = jnp.where(
        mine, prefix[...].astype(F32), pre_in[...].astype(F32)
    ).astype(BF16)
    remote(
        pre_now.at[block(core, 2 * PRE)],
        pre_far.at[block(core, 2 * PRE)],
        p_send.at[1],
        p_recv.at[1],
        (across, tp),
    )

    y_stage(2)
    z_stage(1)
    y_stage(3)
    z_stage(2)
    await_bytes(pre_far.at[block(core, 2 * PRE)], p_recv.at[1])
    remote(
        pre_far.at[block(core, 2 * PRE)],
        pre_far.at[block(core, 2 * PRE)],
        p_send.at[2],
        p_recv.at[2],
        (mate, tp),
    )
    y_stage(4)
    z_stage(3)
    y_stage(5)
    z_stage(4)
    z_stage(5)

    ends = [lengths[0:1, :]]
    for i in range(1, 3):
        ends.append(ends[-1] + lengths[i : i + 1, :])
    query_row = iota((ROWS, ROWS), 1)
    key_row = iota((ROWS, ROWS), 0)
    same = key_row <= query_row
    for end in ends:
        end = jnp.concatenate([end, end], axis=1)
        same = same & ((key_row >= end) == (query_row >= end))
    mask[...] = jnp.where(same, 0.0, NEGATIVE)
    await_bytes(pre_far.at[block(1 - core, 2 * PRE)], p_recv.at[2])
    await_bytes(pre_now.at[pl.ds(0, 2 * PRE)], p_send.at[1])
    here = (hold >> 1) == side
    pre_now[...] = jnp.where(
        here, pre_now[...].astype(F32), pre_far[...].astype(F32)
    ).astype(BF16)
    from_y[...] = turned(to_y[...])
    from_z[...] = turned(to_z[...])

    await_bytes(z_table_in, t_recv.at[2])
    code = compacted(z_table_in[...], cap_z) - 1
    rows = hot(arrival[:, 0:1] == code)
    to_rows[...] = rows
    from_rows[...] = turned(rows)

    def back_z(chunk, result):
        wide = result.shape[1]
        lanes = pl.ds(0, wide)
        bz_out[chunk, :, 0:wide] = dot(from_rows[...], result).astype(BF16)
        for k in (4, 3, 5, 2, 6, 1, 7):
            remote(
                bz_out.at[chunk, block(z_peer(k), cap_z), lanes],
                bz_in.at[chunk, block(plane, cap_z), lanes],
                bz_send.at[chunk],
                bz_recv.at[chunk],
                at_z(k),
            )
        local(
            bz_out.at[chunk, block(plane, cap_z), lanes],
            bz_in.at[chunk, block(plane, cap_z), lanes],
            bz_recv.at[chunk],
        )

    def back_y(chunk):
        wide = WIDTHS[chunk % 4]
        lanes = pl.ds(0, wide)
        await_bytes(bz_in.at[chunk, :, lanes], bz_recv.at[chunk])
        by_out[chunk, :, 0:wide] = dot(from_z[...], bz_in[chunk, :, 0:wide]).astype(BF16)
        for k in range(1, PLANE):
            remote(
                by_out.at[chunk, block(y_peer(k), cap_y), lanes],
                by_in.at[chunk, block(spot, cap_y), lanes],
                by_send.at[chunk],
                by_recv.at[chunk],
                at_y(k),
            )
        local(
            by_out.at[chunk, block(spot, cap_y), lanes],
            by_in.at[chunk, block(spot, cap_y), lanes],
            by_recv.at[chunk],
        )

    def back_x(chunk):
        kh, part = chunk // 4, chunk % 4
        wide = WIDTHS[part]
        lanes = pl.ds(0, wide)
        await_bytes(by_in.at[chunk, :, lanes], by_recv.at[chunk])
        bx_out[chunk, :, 0:wide] = dot(from_y[...], by_in[chunk, :, 0:wide]).astype(BF16)
        head = tp * (KH * RATIO) + kh * RATIO
        if part < 3:
            first = head if part == 0 else head + 2 * part - 1
            parts = ((grad_query, first, wide // D),)
        else:
            parts = ((grad_key, tp * KH + kh, 1), (grad_value, tp * KH + kh, 1))
        for k in range(TP):
            lane = 0
            for target, head, heads in parts:
                src = bx_out.at[chunk, block(x_peer(k), SEND), pl.ds(lane, heads * D)]
                dst = target.at[:, pl.ds(pl.multiple_of(head * D, D), heads * D)]
                if k == 0:
                    local(src, dst, bx_recv.at[chunk])
                else:
                    remote(src, dst, bx_send.at[chunk], bx_recv.at[chunk], at_x(k))
                lane += heads * D

    def reduce_core(kh):
        remote(acc.at[kh, 1 - core], acc_in.at[kh], a_send.at[kh, 0], a_recv.at[kh, 0], (mate, tp))

    def reduce_side(kh):
        await_bytes(acc_in.at[kh], a_recv.at[kh, 0])
        chip[kh] = acc[kh, core] + acc_in[kh]
        remote(chip.at[kh], chip_in.at[kh], a_send.at[kh, 1], a_recv.at[kh, 1], (across, tp))

    def reduce_end(kh):
        await_bytes(chip_in.at[kh], a_recv.at[kh, 1])
        whole = chip[kh] + chip_in[kh]
        total[kh, 0] = jnp.where(hold == 2 * side + core, whole, 0.0)
        total[kh, 1] = jnp.where(hold == 2 * side + 1 - core, whole, 0.0)
        local(total.at[kh, 0], grad_prefix.at[core, kh], a_recv.at[kh, 2])
        remote(
            total.at[kh, 1], grad_prefix.at[core, kh], a_send.at[kh, 2], a_recv.at[kh, 3], (mate, tp)
        )

    def tokens(chunk):
        await_bytes(z_in.at[chunk], z_recv.at[chunk])
        return dot(to_rows[...], z_in[chunk]).astype(BF16)

    def attend(keys, values, keys_t, queries, grads, key_grad, value_grad):
        scores = dot_nt(keys, queries) * SCALE
        scores = jnp.concatenate([scores[:PRE], scores[PRE:] + mask[...]], axis=0)
        weights = jnp.exp(scores - jnp.max(scores, axis=0, keepdims=True))
        probability = weights * (1.0 / jnp.sum(weights, axis=0, keepdims=True))
        grad_prob = dot_nt(values, grads)
        delta = jnp.sum(probability * grad_prob, axis=0, keepdims=True)
        dscore = (probability * (grad_prob - delta)).astype(BF16)
        key_part = dot(dscore, queries)
        value_part = dot(probability.astype(BF16), grads)
        query_grad = (jnp.transpose(dot(keys_t, dscore)) * SCALE).astype(BF16)
        if key_grad is None:
            return query_grad, key_part, value_part
        return query_grad, key_grad + key_part, value_grad + value_part

    later = []
    for kh in range(KH):
        base = kh * 3
        got = tokens(base)
        lower = kh * PRE
        keys = jnp.concatenate([pre_now[lower : lower + PRE], got[:, 0:D]], axis=0)
        values = jnp.concatenate(
            [pre_now[KH * PRE + lower : KH * PRE + lower + PRE], got[:, D : 2 * D]], axis=0
        )
        keys_t = jnp.transpose(keys.astype(F32)).astype(BF16)
        key_grad = value_grad = None
        for part in range(3):
            if part == 0:
                pairs = ((got[:, 2 * D : 3 * D], got[:, 3 * D :]),)
            else:
                got = tokens(base + part)
                pairs = ((got[:, :D], got[:, 2 * D : 3 * D]), (got[:, D : 2 * D], got[:, 3 * D :]))
            results = []
            for queries, grads in pairs:
                result, key_grad, value_grad = attend(
                    keys, values, keys_t, queries, grads, key_grad, value_grad
                )
                results.append(result)
            whole = results[0] if part == 0 else jnp.concatenate(results, axis=1)
            back_z(kh * 4 + part, whole)
            if kh == 1:
                back_y(part)
                if part > 0:
                    back_x(part - 1)
        own = [(key_grad[PRE:] * SCALE).astype(BF16), value_grad[PRE:].astype(BF16)]
        back_z(kh * 4 + 3, jnp.concatenate(own, axis=1))
        acc[kh, 0] = key_grad[:PRE] * SCALE
        acc[kh, 1] = value_grad[:PRE]
        reduce_core(kh)
        if kh == 1:
            reduce_side(0)

    back_y(3)
    back_x(2)
    reduce_side(1)
    back_y(4)
    back_x(3)
    reduce_end(0)
    back_y(5)
    back_x(4)
    back_y(6)
    back_x(5)
    reduce_end(1)
    back_y(7)
    back_x(6)
    back_x(7)

    for i in range(TP - 1):
        await_bytes(route, t_send.at[0])
    for i, ref in ((1, y_table_out), (2, z_table_out)):
        await_bytes(ref.at[:, pl.ds(0, 7 * PITCH)], t_send.at[i])
    for chunk in range(CHUNKS):
        await_bytes(x_in.at[chunk, pl.ds(0, 3 * SEND)], x_send.at[chunk])
        await_bytes(y_out.at[chunk, pl.ds(0, 7 * cap_y)], y_send.at[chunk])
        await_bytes(z_out.at[chunk, pl.ds(0, 7 * cap_z)], z_send.at[chunk])
    for chunk in range(BACKS):
        lanes = pl.ds(0, WIDTHS[chunk % 4])
        await_bytes(bz_out.at[chunk, pl.ds(0, 7 * cap_z), lanes], bz_send.at[chunk])
        await_bytes(by_out.at[chunk, pl.ds(0, 7 * cap_y), lanes], by_send.at[chunk])
        await_bytes(bx_out.at[chunk, pl.ds(0, 3 * SEND), lanes], bx_send.at[chunk])
        await_bytes(bx_out.at[chunk, :, lanes], bx_recv.at[chunk])
    await_bytes(prefix, p_send.at[0])
    await_bytes(pre_now.at[pl.ds(0, 2 * PRE)], p_send.at[2])
    for kh in range(KH):
        await_bytes(acc_in.at[kh], a_send.at[kh, 0])
        await_bytes(chip.at[kh], a_send.at[kh, 1])
        await_bytes(chip.at[kh], a_send.at[kh, 2])
        await_bytes(chip.at[kh], a_recv.at[kh, 2])
        await_bytes(chip.at[kh], a_recv.at[kh, 3])


def whole_step(cap_y, cap_z, operands):
    def vmem(*shape, dtype=BF16):
        return pltpu.VMEM(shape, dtype)

    dma = pltpu.SemaphoreType.DMA
    in_vmem = pl.BlockSpec(memory_space=pltpu.VMEM)
    anywhere = pl.BlockSpec(memory_space=pl.ANY)
    return pl.pallas_call(
        functools.partial(kernel, cap_y, cap_z),
        out_shape=(
            jax.ShapeDtypeStruct((SEND, TP * KH * RATIO * D), BF16),
            jax.ShapeDtypeStruct((SEND, TP * KH * D), BF16),
            jax.ShapeDtypeStruct((SEND, TP * KH * D), BF16),
            jax.ShapeDtypeStruct((2, KH, PRE, D), F32),
        ),
        in_specs=[anywhere] * 4 + [in_vmem] * 5,
        out_specs=(anywhere,) * 4,
        scratch_shapes=[
            vmem(TP - 1, 8, ROWS, dtype=I32),
            vmem(8, 8 * PITCH, dtype=F32),
            vmem(8, 8 * PITCH, dtype=F32),
            vmem(8, 8 * PITCH, dtype=F32),
            vmem(8, 8 * PITCH, dtype=F32),
            vmem(CHUNKS, ROWS, WIDE),
            vmem(CHUNKS, 8 * cap_y, WIDE),
            vmem(CHUNKS, 8 * cap_y, WIDE),
            vmem(CHUNKS, 8 * cap_z, WIDE),
            vmem(CHUNKS, 8 * cap_z, WIDE),
            vmem(BACKS, 8 * cap_z, BACK),
            vmem(BACKS, 8 * cap_z, BACK),
            vmem(BACKS, 8 * cap_y, BACK),
            vmem(BACKS, 8 * cap_y, BACK),
            vmem(BACKS, ROWS, BACK),
            vmem(2 * KH * PRE, D),
            vmem(2 * KH * PRE, D),
            vmem(2 * KH * PRE, D),
            vmem(8 * cap_y, ROWS),
            vmem(8 * cap_z, 8 * cap_y),
            vmem(ROWS, 8 * cap_z),
            vmem(ROWS, 8 * cap_y),
            vmem(8 * cap_y, 8 * cap_z),
            vmem(8 * cap_z, ROWS),
            vmem(ROWS, ROWS, dtype=F32),
            vmem(KH, 2, PRE, D, dtype=F32),
            vmem(KH, PRE, D, dtype=F32),
            vmem(KH, PRE, D, dtype=F32),
            vmem(KH, PRE, D, dtype=F32),
            vmem(KH, 2, PRE, D, dtype=F32),
            dma((3,)),
            dma((3,)),
            dma((CHUNKS,)),
            dma((CHUNKS,)),
            dma((CHUNKS,)),
            dma((CHUNKS,)),
            dma((CHUNKS,)),
            dma((CHUNKS,)),
            dma((BACKS,)),
            dma((BACKS,)),
            dma((BACKS,)),
            dma((BACKS,)),
            dma((BACKS,)),
            dma((BACKS,)),
            dma((3,)),
            dma((3,)),
            dma((KH, 3)),
            dma((KH, 4)),
        ],
        compiler_params=pltpu.CompilerParams(
            collective_id=0, has_side_effects=True, vmem_limit_bytes=60 * 2**20
        ),
    )(*operands)


def body(
    roll_query, roll_key, roll_value, roll_cotangent, route, arrival, lengths, prefix_kv, owner
):
    tp = lax.axis_index("tp")
    group = lax.axis_index("grp") // TP
    line = jnp.arange(ROWS, dtype=I32) // SEND
    routes = jnp.broadcast_to(jnp.where(line == tp, jnp.tile(route, TP), 0)[None], (8, ROWS))
    arrivals = jnp.broadcast_to(arrival[:, None], (ROWS, D))
    sizes = jnp.broadcast_to(
        jnp.concatenate([lengths[0], lengths[0]])[:, None].astype(I32), (8, D)
    )
    held = jnp.transpose(prefix_kv[0].reshape(PRE, 2, KH, D), (1, 2, 0, 3))
    held = held.reshape(2 * KH * PRE, D)
    holder = jnp.broadcast_to(owner[group], (8, D))
    operands = (
        roll_query,
        roll_key,
        roll_value,
        roll_cotangent,
        routes,
        arrivals,
        sizes,
        held,
        holder,
    )
    grad_query, grad_key, grad_value, grad_prefix = whole_step(64, 64, operands)
    grad_prefix = jnp.transpose(grad_prefix, (2, 0, 1, 3)).reshape(1, PRE, 2, KH * D)
    return grad_query, grad_key, grad_value, grad_prefix


def solution(mesh):
    return jax.shard_map(
        body,
        mesh=mesh,
        in_specs=(
            P(("grp", "tp"), None),
            P(("grp", "tp"), None),
            P(("grp", "tp"), None),
            P(("grp", "tp"), None),
            P(("grp", "tp")),
            P("grp"),
            P("grp", None),
            P("grp", None, None, "tp"),
            P(),
        ),
        out_specs=(
            P(("grp", "tp"), None),
            P(("grp", "tp"), None),
            P(("grp", "tp"), None),
            P("grp", None, None, "tp"),
        ),
        check_vma=False,
    )
```

profile of v0, /device:TPU:1, one launch (start us, length us, event | category | flops | bytes accessed | tf_op | source)
XLA Modules:
  0.0 162.2 jit_solution(18164274105392291428)
XLA Ops:
  0.6 0.0 copy-start.5
  0.7 0.6 copy-done.5
  1.3 0.6 dynamic_slice.3
  1.9 0.0 copy-start.6
  1.9 0.7 copy-done.6
  2.5 0.0 copy-start.4
  2.5 0.1 pad_add_fusion
  2.6 0.6 copy-done.4
  3.2 0.1 tile.10
  3.3 0.7 broadcast_in_dim.12.lengths
  4.0 1.2 broadcast_in_dim.13.holder
  5.2 0.0 copy-start.3
  5.2 0.6 broadcast_in_dim.10.route
  5.8 0.1 copy-done.3
  5.9 0.8 broadcast_in_dim.11.arrival
  6.6 2.3 %reshape_squeeze.3 = bf16[512,2,2,128]{3,2,1,0:T(2,128)(2,1)S(1)} reshape(bf16[1,512,2,256]{3,2,1,0:T(2,128)(2,1)} %param.16) | data formatting | bytes 1048576 | tf_op jit(solution)/shard_map/reshape;squeeze | solution.py:635
  8.9 0.9 copy.14
  9.8 146.9 %shard_map.120 = (bf16[64,5120]{1,0:T(8,128)(2,1)}, bf16[64,1024]{1,0:T(8,128)(2,1)}, bf16[64,1024]{1,0:T(8,128)(2,1)}, f32[2,2,512,128]{3,2,1,0:T(8,128)}) custom-call(bf16[64,5120]{1,0:T(8,128)(2,1)} %query.1, bf16[64,1024]{1,0:T(8,128)(2,1)} %key.1, bf16[64,1024]{1,0:T(8,128)(2,1)} %value.1, bf16[64,5120]{1,0:T(8,128)(2,1)} %cotangent.1, ...), custom_call_target="tpu_custom_call" | custom-call | tf_op jit(solution)/shard_map/pallas_call | solution.py:558
  156.7 1.6 copy.15
  158.3 0.0 copy-start
  158.3 1.3 copy.16
  159.6 0.0 copy-done
  159.6 0.0 copy-start.2
  159.6 0.8 copy.20
  160.4 0.2 copy-done.2
  160.6 0.0 copy-start.1
  160.6 0.7 copy.21
  161.3 0.3 copy-done.1
  161.6 0.7 copy.22
  (2 shorter events, 0.0 us)
Async XLA Ops:
  0.6 0.7 copy-start.5
  1.9 0.7 copy-start.6
  2.5 0.7 copy-start.4
  5.2 0.7 copy-start.3
  158.3 1.3 copy-start
  159.6 1.0 copy-start.2
  160.6 1.0 copy-start.1
where the time goes:
time: 162 us
  Pallas kernels  147 us (91%)
  local copies, waits for them, and re-layouts  14.5 us (9%)
    pallas_call x1, Pallas kernels, whole_step(): pl.pallas_call(functools.partial(kernel, cap_y, cap_z), out_shape=(jax.Sh...  147 us
    unnamed x18, local copies, waits for them, and re-layouts  5.9 us

commit v1 on v0

--- a/solution.py
+++ b/solution.py
@@ -55,15 +55,20 @@
     kind, valid = kind[0:1], valid[0:1]
     slot = jnp.where(valid & (rank < limit), kind * limit + rank, -1)
     table = jnp.where(valid & (rank < limit), kind * PITCH + rank, -1)
-    return slot, table
-
-
-def tabulate(code, table, lanes):
+    over = jnp.max(jnp.where(valid & (rank >= limit), 1.0, 0.0), axis=1, keepdims=True)
+    return slot, table, over
+
+
+def tabulate(code, table, over, lanes):
     sub = iota((8, lanes), 0)
     high, low = code >> 7, code & 127
     parts = jnp.where(sub == 0, high, jnp.where(sub == 1, low, 0)).astype(F32).astype(BF16)
     spread = hot(iota((8 * PITCH, lanes), 0) == table)
-    return dot_nt(parts, spread)
+    return jnp.where(iota((8, 8 * PITCH), 0) == 2, over, dot_nt(parts, spread))
+
+
+def flagged(table):
+    return jnp.max(table[2:3], axis=1, keepdims=True)
 
 
 def compacted(table, limit):
@@ -99,11 +104,14 @@
     grad_key,
     grad_value,
     grad_prefix,
+    overflow,
     x_table,
     y_table_out,
     y_table_in,
     z_table_out,
     z_table_in,
+    flag_out,
+    flag_in,
     x_in,
     y_out,
     y_in,
@@ -245,9 +253,9 @@
     line = iota((8, ROWS), 1) // SEND
     number = grp * (2 * TP) + line * 2 + (routes & 1)
     code = ((trainer >> 3) * 512 + number + 1)[0:1]
-    slot, table = place(trainer & 7, trainer >= 0, ROWS, cap_y)
+    slot, table, over = place(trainer & 7, trainer >= 0, ROWS, cap_y)
     to_y[...] = hot(iota((8 * cap_y, ROWS), 0) == slot)
-    y_table_out[...] = tabulate(code, table, ROWS)
+    y_table_out[...] = tabulate(code, table, over, ROWS)
     for k in range(1, PLANE):
         remote(
             y_table_out.at[:, block(y_peer(k), PITCH)],
@@ -301,9 +309,10 @@
     code = compacted(y_table_in[...], cap_y)
     lanes = 8 * cap_y
     code8 = jnp.broadcast_to(code, (8, lanes))
-    slot, table = place((code8 - 1) >> 9, code8 > 0, lanes, cap_z)
+    slot, table, over = place((code8 - 1) >> 9, code8 > 0, lanes, cap_z)
     to_z[...] = hot(iota((8 * cap_z, lanes), 0) == slot)
-    z_table_out[...] = tabulate(((code - 1) & 511) + 1, table, lanes)
+    over = jnp.maximum(over, flagged(y_table_in[...]))
+    z_table_out[...] = tabulate(((code - 1) & 511) + 1, table, over, lanes)
     for k in range(1, PLANE):
         remote(
             z_table_out.at[:, block(z_peer(k), PITCH)],
@@ -371,6 +380,9 @@
 
     await_bytes(z_table_in, t_recv.at[2])
     code = compacted(z_table_in[...], cap_z) - 1
+    flag_out[...] = jnp.broadcast_to(flagged(z_table_in[...]), (8, PITCH))
+    for k in range(1, PLANE):
+        remote(flag_out, flag_in.at[k - 1], t_send.at[3], t_recv.at[3], at_y(k))
     rows = hot(arrival[:, 0:1] == code)
     to_rows[...] = rows
     from_rows[...] = turned(rows)
@@ -522,10 +534,13 @@
     reduce_end(1)
     back_y(7)
     back_x(6)
+    await_bytes(flag_in, t_recv.at[3])
+    overflow[...] = jnp.maximum(flag_out[...], jnp.max(flag_in[...], axis=0))
     back_x(7)
 
     for i in range(TP - 1):
         await_bytes(route, t_send.at[0])
+    await_bytes(flag_in, t_send.at[3])
     for i, ref in ((1, y_table_out), (2, z_table_out)):
         await_bytes(ref.at[:, pl.ds(0, 7 * PITCH)], t_send.at[i])
     for chunk in range(CHUNKS):
@@ -548,7 +563,7 @@
         await_bytes(chip.at[kh], a_recv.at[kh, 3])
 
 
-def whole_step(cap_y, cap_z, operands):
+def whole_step(cap_y, cap_z, number, operands):
     def vmem(*shape, dtype=BF16):
         return pltpu.VMEM(shape, dtype)
 
@@ -562,15 +577,18 @@
             jax.ShapeDtypeStruct((SEND, TP * KH * D), BF16),
             jax.ShapeDtypeStruct((SEND, TP * KH * D), BF16),
             jax.ShapeDtypeStruct((2, KH, PRE, D), F32),
+            jax.ShapeDtypeStruct((8, PITCH), F32),
         ),
         in_specs=[anywhere] * 4 + [in_vmem] * 5,
-        out_specs=(anywhere,) * 4,
+        out_specs=(anywhere,) * 4 + (in_vmem,),
         scratch_shapes=[
             vmem(TP - 1, 8, ROWS, dtype=I32),
             vmem(8, 8 * PITCH, dtype=F32),
             vmem(8, 8 * PITCH, dtype=F32),
             vmem(8, 8 * PITCH, dtype=F32),
             vmem(8, 8 * PITCH, dtype=F32),
+            vmem(8, PITCH, dtype=F32),
+            vmem(PLANE - 1, 8, PITCH, dtype=F32),
             vmem(CHUNKS, ROWS, WIDE),
             vmem(CHUNKS, 8 * cap_y, WIDE),
             vmem(CHUNKS, 8 * cap_y, WIDE),
@@ -596,8 +614,8 @@
             vmem(KH, PRE, D, dtype=F32),
             vmem(KH, PRE, D, dtype=F32),
             vmem(KH, 2, PRE, D, dtype=F32),
-            dma((3,)),
-            dma((3,)),
+            dma((4,)),
+            dma((4,)),
             dma((CHUNKS,)),
             dma((CHUNKS,)),
             dma((CHUNKS,)),
@@ -616,7 +634,7 @@
             dma((KH, 4)),
         ],
         compiler_params=pltpu.CompilerParams(
-            collective_id=0, has_side_effects=True, vmem_limit_bytes=60 * 2**20
+            collective_id=number, has_side_effects=True, vmem_limit_bytes=60 * 2**20
         ),
     )(*operands)
 
@@ -646,7 +664,12 @@
         held,
         holder,
     )
-    grad_query, grad_key, grad_value, grad_prefix = whole_step(64, 64, operands)
+    *quick, overflow = whole_step(48, 48, 0, operands)
+    grad_query, grad_key, grad_value, grad_prefix = lax.cond(
+        overflow[0, 0] > 0.5,
+        lambda: tuple(whole_step(64, 64, 1, operands)[:4]),
+        lambda: tuple(quick),
+    )
     grad_prefix = jnp.transpose(grad_prefix, (2, 0, 1, 3)).reshape(1, PRE, 2, KH * D)
     return grad_query, grad_key, grad_value, grad_prefix
 

time: 162 us -> 137 us (0.85)
  Pallas kernels: 147 us -> 120 us
    pallas_call x1, Pallas kernels: 147 us -> 120 us  [whole_step(): pl.pallas_call(functools.partial(kernel, cap_y, cap_z), out_shape=(jax.Sh...]
    reshape x0 -> x1, local copies, waits for them, and re-layouts: none -> 2.17 us  [body(): jnp.transpose(grad_prefix, (2, 0, 1, 3)).reshape(1, PRE, 2, KH * D)]
    unnamed x18 -> x21, local copies, waits for them, and re-layouts: 5.9 us -> 6.02 us
where the time goes in v1:
time: 137 us; the launch traced here: 136 us
  Pallas kernels  120 us (88%)
  local copies, waits for them, and re-layouts  14.1 us (10%)
  between operations  1.43 us (1%)
    pallas_call x1, Pallas kernels, whole_step(): pl.pallas_call(functools.partial(kernel, cap_y, cap_z), out_shape=(jax.Sh...  120 us
    unnamed x21, local copies, waits for them, and re-layouts  6.02 us

profile of v1, /device:TPU:1, one launch (start us, length us, event | category | flops | bytes accessed | tf_op | source)
XLA Modules:
  0.0 136.3 jit_solution(14383062411458646684)
XLA Ops:
  0.6 0.0 copy-start.7
  0.7 0.6 copy-done.7
  1.3 0.6 dynamic_slice.3
  1.9 0.0 copy-start.8
  1.9 0.7 copy-done.8
  2.5 0.1 pad_add_fusion
  2.6 0.6 copy-done.6
  3.2 0.1 tile.10
  3.3 0.1 broadcast_in_dim.12.lengths
  3.4 0.6 broadcast_in_dim.13.holder
  4.0 0.0 copy-start.5
  4.0 0.7 copy-done.5
  4.7 0.1 broadcast_in_dim.11.arrival
  4.8 0.0 copy-start.1
  4.8 2.4 %reshape_squeeze.3 = bf16[512,2,2,128]{3,2,1,0:T(2,128)(2,1)S(1)} reshape(bf16[1,512,2,256]{3,2,1,0:T(2,128)(2,1)} %param.18) | data formatting | bytes 1048576 | tf_op jit(solution)/shard_map/reshape;squeeze | solution.py:653
  7.2 0.0 copy-start
  7.2 0.0 copy-start.2
  7.2 0.0 copy-start.3
  7.2 0.1 copy.13
  7.3 0.0 copy-done.1
  7.3 1.0 copy-done
  8.3 0.0 copy-done.2
  8.3 0.0 copy-done.3
  8.3 120.5 %shard_map.120 = (bf16[64,5120]{1,0:T(8,128)(2,1)S(1)}, bf16[64,1024]{1,0:T(8,128)(2,1)S(1)}, bf16[64,1024]{1,0:T(8,128)(2,1)}, f32[2,2,512,128]{3,2,1,0:T(8,128)S(1)}, f32[8,128]{1,0:T(8,128)}) custom-call(bf16[64,5120]{1,0:T(8,128)(2,1)S(1)} %copy-done, bf16[64,1024]{1,0:T(8,128)(2,1)S(1)} %copy-done.2, bf16[64,1024]{1,0:T(8,128)(2,1)S(1)} %copy-done.3, ...), custom_call_target="tpu_custom_call" | custom-call | tf_op jit(solution)/shard_map/pallas_call | solution.py:573
  128.8 1.2 slice.3
  130.6 0.3 conditional.1
  130.9 0.8 copy.14
  131.7 2.2 %reshape.41 = f32[1,512,2,256]{3,2,1,0:T(2,128)} reshape(f32[512,2,2,128]{3,2,1,0:T(2,128)S(1)} %copy.14) | data formatting | bytes 2097152 | tf_op jit(solution)/shard_map/reshape | solution.py:673
  133.9 0.8 copy.26
  134.7 0.7 copy.27
  135.4 0.3 copy-done.4
  135.7 0.7 copy.28
  (5 shorter events, 0.0 us)
Async XLA Ops:
  0.6 0.7 copy-start.7
  1.9 0.7 copy-start.8
  2.5 0.7 copy-start.6
  4.0 0.7 copy-start.5
  4.8 2.5 %copy-start.1 = (bf16[64,5120]{1,0:T(8,128)(2,1)S(1)}, bf16[64,5120]{1,0:T(8,128)(2,1)}, u32[]{:S(2)}) copy-start(bf16[64,5120]{1,0:T(8,128)(2,1)} %cotangent.1) | copy-start | bytes 1966084
  7.2 1.1 copy-start
  7.2 1.1 copy-start.2
  7.2 1.1 copy-start.3
  134.7 1.0 copy-start.4

commit v2 on v1

--- a/solution.py
+++ b/solution.py
@@ -17,9 +17,30 @@
 ROWS = 256
 SEND = 64
 PRE = 512
-CHUNKS = 6
+FORWARD = (
+    (("k", 0, 1), ("v", 0, 1)),
+    (("q", 0, 1), ("c", 0, 1)),
+    (("q", 1, 2), ("c", 1, 2)),
+    (("q", 3, 2), ("c", 3, 2)),
+    (("k", 1, 1), ("v", 1, 1), ("q", 5, 1), ("c", 5, 1)),
+    (("q", 6, 2), ("c", 6, 2)),
+    (("q", 8, 1), ("c", 8, 1)),
+    (("q", 9, 1), ("c", 9, 1)),
+)
+BACKWARD = (
+    (("q", 0, 1),),
+    (("q", 1, 2),),
+    (("q", 3, 2),),
+    (("k", 0, 1), ("v", 0, 1)),
+    (("q", 5, 1),),
+    (("q", 6, 2),),
+    (("q", 8, 1),),
+    (("q", 9, 1),),
+    (("k", 1, 1), ("v", 1, 1)),
+)
+CHUNKS = len(FORWARD)
+BACKS = len(BACKWARD)
 WIDE = 512
-BACKS = 8
 BACK = 256
 PITCH = 128
 NEGATIVE = -1e30
@@ -27,7 +48,21 @@
 F32 = jnp.float32
 BF16 = jnp.bfloat16
 I32 = jnp.int32
-WIDTHS = (128, 256, 256, 256)
+AHEAD = 2
+PROMPT = 5
+
+
+def width(chunk):
+    return D * sum(heads for _, _, heads in chunk)
+
+
+def found(chunks, kind, head):
+    for number, chunk in enumerate(chunks):
+        lane = 0
+        for name, first, heads in chunk:
+            if name == kind and first <= head < first + heads:
+                return number, lane + (head - first) * D
+            lane += heads * D
 
 
 def iota(shape, dim):
@@ -71,13 +106,18 @@
     return jnp.max(table[2:3], axis=1, keepdims=True)
 
 
-def compacted(table, limit):
+def compacted(table, limit, column=False):
     lanes = 8 * limit
     lane = iota((8 * PITCH, lanes), 1)
     target = lane
     for i in range(1, 8):
         target = target + jnp.where(lane >= i * limit, PITCH - limit, 0)
     pick = hot(iota((8 * PITCH, lanes), 0) == target)
+    if column:
+        parts = lax.dot_general(
+            pick, table.astype(BF16), (((0,), (1,)), ((), ())), preferred_element_type=F32
+        )
+        return (parts[:, 0:1] * 128.0 + parts[:, 1:2]).astype(I32)
     parts = dot(table.astype(BF16), pick)
     return (parts[0:1] * 128.0 + parts[1:2]).astype(I32)
 
@@ -99,12 +139,13 @@
     arrival,
     lengths,
     prefix,
-    holder,
+    owner,
     grad_query,
     grad_key,
     grad_value,
     grad_prefix,
     overflow,
+    x_table_out,
     x_table,
     y_table_out,
     y_table_in,
@@ -122,6 +163,8 @@
     by_out,
     by_in,
     bx_out,
+    pre_raw,
+    pre_own,
     pre_in,
     pre_now,
     pre_far,
@@ -137,6 +180,7 @@
     chip,
     chip_in,
     total,
+    total_in,
     t_send,
     t_recv,
     x_send,
@@ -204,6 +248,7 @@
     def await_bytes(ref, sem):
         pltpu.make_async_copy(ref, ref, sem).wait()
 
+    local(prefix.at[0], pre_raw, p_recv.at[3])
     entry = pltpu.get_barrier_semaphore()
     for k in range(1, TP):
         pl.semaphore_signal(entry, inc=1, device_id=at_x(k), device_id_type=MESH)
@@ -213,28 +258,23 @@
         pl.semaphore_signal(entry, inc=1, device_id=at_z(k), device_id_type=MESH)
     pl.semaphore_wait(entry, TP - 1 + 2 * (PLANE - 1))
 
+    x_table_out[...] = jnp.broadcast_to(route[...].reshape(1, SEND), (8, SEND)).astype(F32)
     for k in range(1, TP):
-        remote(route, x_table.at[k - 1], t_send.at[0], t_recv.at[0], at_x(k))
-
-    def chunk_parts(chunk, to):
-        kh, part = chunk // 3, chunk % 3
-        head = to * (KH * RATIO) + kh * RATIO
-        if part == 0:
-            return (
-                (key, to * KH + kh, 1),
-                (value, to * KH + kh, 1),
-                (query, head, 1),
-                (cotangent, head, 1),
-            )
-        first = head + 2 * part - 1
-        return ((query, first, 2), (cotangent, first, 2))
+        remote(x_table_out, x_table.at[k - 1], t_send.at[0], t_recv.at[0], at_x(k))
+
+    def place_of(kind, head, device):
+        per = KH if kind in "kv" else KH * RATIO
+        return pl.multiple_of((device * per + head) * D, D)
 
     def x_stage(chunk):
+        if chunk >= CHUNKS:
+            return
+        sources = {"q": query, "k": key, "v": value, "c": cotangent}
         for k in range(TP):
             to = x_peer(k)
             lane = 0
-            for source, head, heads in chunk_parts(chunk, to):
-                src = source.at[:, pl.ds(pl.multiple_of(head * D, D), heads * D)]
+            for kind, head, heads in FORWARD[chunk]:
+                src = sources[kind].at[:, pl.ds(place_of(kind, head, to), heads * D)]
                 dst = x_in.at[chunk, block(tp, SEND), pl.ds(lane, heads * D)]
                 if k == 0:
                     local(src, dst, x_recv.at[chunk])
@@ -242,13 +282,25 @@
                     remote(src, dst, x_send.at[chunk], x_recv.at[chunk], at_x(k))
                 lane += heads * D
 
-    x_stage(0)
-    remote(prefix, pre_in, p_send.at[0], p_recv.at[0], (mate, tp))
-    for chunk in range(1, CHUNKS):
+    for chunk in range(AHEAD):
         x_stage(chunk)
 
+    await_bytes(pre_raw, p_recv.at[3])
+    for kv in range(2):
+        part = pre_raw[:, kv, :]
+        for kh in range(KH):
+            lower = (kv * KH + kh) * PRE
+            pre_own[lower : lower + PRE] = part[:, kh * D : (kh + 1) * D]
+    remote(pre_own, pre_in, p_send.at[0], p_recv.at[0], (mate, tp))
+
     await_bytes(x_table, t_recv.at[0])
-    routes = route[...] + x_table[0] + x_table[1] + x_table[2]
+    routes = jnp.zeros((8, ROWS), F32)
+    for k in range(TP):
+        begin = lax.rem(tp + TP - k, TP) * SEND
+        spread = hot(iota((SEND, ROWS), 0) + begin == iota((SEND, ROWS), 1))
+        heard = x_table_out[...] if k == 0 else x_table[k - 1]
+        routes = routes + dot(heard.astype(BF16), spread)
+    routes = routes.astype(I32)
     trainer = routes >> 1
     line = iota((8, ROWS), 1) // SEND
     number = grp * (2 * TP) + line * 2 + (routes & 1)
@@ -269,36 +321,41 @@
     )
 
     def y_stage(chunk):
-        await_bytes(x_in.at[chunk], x_recv.at[chunk])
-        y_out[chunk] = dot(to_y[...], x_in[chunk]).astype(BF16)
+        wide = width(FORWARD[chunk])
+        lanes = pl.ds(0, wide)
+        await_bytes(x_in.at[chunk, :, lanes], x_recv.at[chunk])
+        x_stage(chunk + AHEAD)
+        y_out[chunk, :, 0:wide] = dot(to_y[...], x_in[chunk, :, 0:wide]).astype(BF16)
         for k in range(1, PLANE):
             remote(
-                y_out.at[chunk, block(y_peer(k), cap_y)],
-                y_in.at[chunk, block(spot, cap_y)],
+                y_out.at[chunk, block(y_peer(k), cap_y), lanes],
+                y_in.at[chunk, block(spot, cap_y), lanes],
                 y_send.at[chunk],
                 y_recv.at[chunk],
                 at_y(k),
             )
         local(
-            y_out.at[chunk, block(spot, cap_y)],
-            y_in.at[chunk, block(spot, cap_y)],
+            y_out.at[chunk, block(spot, cap_y), lanes],
+            y_in.at[chunk, block(spot, cap_y), lanes],
             y_recv.at[chunk],
         )
 
     def z_stage(chunk):
-        await_bytes(y_in.at[chunk], y_recv.at[chunk])
-        z_out[chunk] = dot(to_z[...], y_in[chunk]).astype(BF16)
+        wide = width(FORWARD[chunk])
+        lanes = pl.ds(0, wide)
+        await_bytes(y_in.at[chunk, :, lanes], y_recv.at[chunk])
+        z_out[chunk, :, 0:wide] = dot(to_z[...], y_in[chunk, :, 0:wide]).astype(BF16)
         for k in (4, 3, 5, 2, 6, 1, 7):
             remote(
-                z_out.at[chunk, block(z_peer(k), cap_z)],
-                z_in.at[chunk, block(plane, cap_z)],
+                z_out.at[chunk, block(z_peer(k), cap_z), lanes],
+                z_in.at[chunk, block(plane, cap_z), lanes],
                 z_send.at[chunk],
                 z_recv.at[chunk],
                 at_z(k),
             )
         local(
-            z_out.at[chunk, block(plane, cap_z)],
-            z_in.at[chunk, block(plane, cap_z)],
+            z_out.at[chunk, block(plane, cap_z), lanes],
+            z_in.at[chunk, block(plane, cap_z), lanes],
             z_recv.at[chunk],
         )
 
@@ -327,65 +384,61 @@
 
     z_stage(0)
 
-    hold = holder[0:1, :]
-    await_bytes(pre_in, p_recv.at[0])
-    mine = (hold & 1) == core
-    pre_now[...] = jnp.where(
-        mine, prefix[...].astype(F32), pre_in[...].astype(F32)
-    ).astype(BF16)
-    remote(
-        pre_now.at[block(core, 2 * PRE)],
-        pre_far.at[block(core, 2 * PRE)],
-        p_send.at[1],
-        p_recv.at[1],
-        (across, tp),
-    )
-
-    y_stage(2)
-    z_stage(1)
-    y_stage(3)
-    z_stage(2)
-    await_bytes(pre_far.at[block(core, 2 * PRE)], p_recv.at[1])
-    remote(
-        pre_far.at[block(core, 2 * PRE)],
-        pre_far.at[block(core, 2 * PRE)],
-        p_send.at[2],
-        p_recv.at[2],
-        (mate, tp),
-    )
-    y_stage(4)
-    z_stage(3)
-    y_stage(5)
-    z_stage(4)
-    z_stage(5)
-
-    ends = [lengths[0:1, :]]
-    for i in range(1, 3):
-        ends.append(ends[-1] + lengths[i : i + 1, :])
+    hold = owner[grp // TP]
+
+    def prompt_across():
+        await_bytes(pre_in, p_recv.at[0])
+        mine = (hold & 1) == core
+        pre_now[...] = jnp.where(mine, pre_own[...].astype(F32), pre_in[...].astype(F32)).astype(BF16)
+        remote(
+            pre_now.at[block(core, 2 * PRE)],
+            pre_far.at[block(core, 2 * PRE)],
+            p_send.at[1],
+            p_recv.at[1],
+            (across, tp),
+        )
+
+    def prompt_mate():
+        await_bytes(pre_far.at[block(core, 2 * PRE)], p_recv.at[1])
+        remote(
+            pre_far.at[block(core, 2 * PRE)],
+            pre_far.at[block(core, 2 * PRE)],
+            p_send.at[2],
+            p_recv.at[2],
+            (mate, tp),
+        )
+
+    for chunk in range(2, CHUNKS):
+        y_stage(chunk)
+        z_stage(chunk - 1)
+        if chunk == PROMPT:
+            prompt_across()
+    z_stage(CHUNKS - 1)
+    prompt_mate()
+
     query_row = iota((ROWS, ROWS), 1)
     key_row = iota((ROWS, ROWS), 0)
     same = key_row <= query_row
-    for end in ends:
-        end = jnp.concatenate([end, end], axis=1)
+    end = 0
+    for i in range(3):
+        end = end + lengths[0, i]
         same = same & ((key_row >= end) == (query_row >= end))
     mask[...] = jnp.where(same, 0.0, NEGATIVE)
     await_bytes(pre_far.at[block(1 - core, 2 * PRE)], p_recv.at[2])
     await_bytes(pre_now.at[pl.ds(0, 2 * PRE)], p_send.at[1])
     here = (hold >> 1) == side
-    pre_now[...] = jnp.where(
-        here, pre_now[...].astype(F32), pre_far[...].astype(F32)
-    ).astype(BF16)
+    pre_now[...] = jnp.where(here, pre_now[...].astype(F32), pre_far[...].astype(F32)).astype(BF16)
     from_y[...] = turned(to_y[...])
     from_z[...] = turned(to_z[...])
 
     await_bytes(z_table_in, t_recv.at[2])
-    code = compacted(z_table_in[...], cap_z) - 1
     flag_out[...] = jnp.broadcast_to(flagged(z_table_in[...]), (8, PITCH))
     for k in range(1, PLANE):
         remote(flag_out, flag_in.at[k - 1], t_send.at[3], t_recv.at[3], at_y(k))
-    rows = hot(arrival[:, 0:1] == code)
-    to_rows[...] = rows
-    from_rows[...] = turned(rows)
+    code = compacted(z_table_in[...], cap_z, column=True) - 1
+    rows = hot(code == arrival[...].reshape(1, ROWS))
+    from_rows[...] = rows
+    to_rows[...] = turned(rows)
 
     def back_z(chunk, result):
         wide = result.shape[1]
@@ -406,7 +459,7 @@
         )
 
     def back_y(chunk):
-        wide = WIDTHS[chunk % 4]
+        wide = width(BACKWARD[chunk])
         lanes = pl.ds(0, wide)
         await_bytes(bz_in.at[chunk, :, lanes], bz_recv.at[chunk])
         by_out[chunk, :, 0:wide] = dot(from_z[...], bz_in[chunk, :, 0:wide]).astype(BF16)
@@ -425,22 +478,16 @@
         )
 
     def back_x(chunk):
-        kh, part = chunk // 4, chunk % 4
-        wide = WIDTHS[part]
+        wide = width(BACKWARD[chunk])
         lanes = pl.ds(0, wide)
         await_bytes(by_in.at[chunk, :, lanes], by_recv.at[chunk])
         bx_out[chunk, :, 0:wide] = dot(from_y[...], by_in[chunk, :, 0:wide]).astype(BF16)
-        head = tp * (KH * RATIO) + kh * RATIO
-        if part < 3:
-            first = head if part == 0 else head + 2 * part - 1
-            parts = ((grad_query, first, wide // D),)
-        else:
-            parts = ((grad_key, tp * KH + kh, 1), (grad_value, tp * KH + kh, 1))
+        targets = {"q": grad_query, "k": grad_key, "v": grad_value}
         for k in range(TP):
             lane = 0
-            for target, head, heads in parts:
+            for kind, head, heads in BACKWARD[chunk]:
                 src = bx_out.at[chunk, block(x_peer(k), SEND), pl.ds(lane, heads * D)]
-                dst = target.at[:, pl.ds(pl.multiple_of(head * D, D), heads * D)]
+                dst = targets[kind].at[:, pl.ds(place_of(kind, head, tp), heads * D)]
                 if k == 0:
                     local(src, dst, bx_recv.at[chunk])
                 else:
@@ -455,19 +502,23 @@
         chip[kh] = acc[kh, core] + acc_in[kh]
         remote(chip.at[kh], chip_in.at[kh], a_send.at[kh, 1], a_recv.at[kh, 1], (across, tp))
 
+    def reduce_mate(kh):
+        await_bytes(chip_in.at[kh], a_recv.at[kh, 1])
+        total[kh] = chip[kh] + chip_in[kh]
+        remote(total.at[kh], total_in.at[kh], a_send.at[kh, 2], a_recv.at[kh, 2], (mate, tp))
+
     def reduce_end(kh):
-        await_bytes(chip_in.at[kh], a_recv.at[kh, 1])
-        whole = chip[kh] + chip_in[kh]
-        total[kh, 0] = jnp.where(hold == 2 * side + core, whole, 0.0)
-        total[kh, 1] = jnp.where(hold == 2 * side + 1 - core, whole, 0.0)
-        local(total.at[kh, 0], grad_prefix.at[core, kh], a_recv.at[kh, 2])
-        remote(
-            total.at[kh, 1], grad_prefix.at[core, kh], a_send.at[kh, 2], a_recv.at[kh, 3], (mate, tp)
-        )
+        await_bytes(total_in.at[kh], a_recv.at[kh, 2])
+        mine, theirs = total[kh], total_in[kh]
+        for kv in range(2):
+            whole = jnp.where(core == kv, mine, theirs)
+            whole = jnp.where(hold == 2 * side + core, whole, 0.0)
+            grad_prefix[0, :, kv, kh * D : (kh + 1) * D] = whole
 
     def tokens(chunk):
-        await_bytes(z_in.at[chunk], z_recv.at[chunk])
-        return dot(to_rows[...], z_in[chunk]).astype(BF16)
+        wide = width(FORWARD[chunk])
+        await_bytes(z_in.at[chunk, :, pl.ds(0, wide)], z_recv.at[chunk])
+        return dot(to_rows[...], z_in[chunk, :, 0:wide]).astype(BF16)
 
     def attend(keys, values, keys_t, queries, grads, key_grad, value_grad):
         scores = dot_nt(keys, queries) * SCALE
@@ -484,83 +535,88 @@
             return query_grad, key_part, value_part
         return query_grad, key_grad + key_part, value_grad + value_part
 
-    later = []
+    arrived = {}
+
+    def rows_of(kind, head):
+        chunk, lane = found(FORWARD, kind, head)
+        if chunk not in arrived:
+            arrived[chunk] = tokens(chunk)
+        return arrived[chunk][:, lane : lane + D]
+
+    done = {}
+
+    def finish(kind, head, value):
+        done[kind, head] = value
+        chunk, _ = found(BACKWARD, kind, head)
+        names = [(k, h) for k, first, heads in BACKWARD[chunk] for h in range(first, first + heads)]
+        if all(name in done for name in names):
+            parts = [done[name] for name in names]
+            back_z(chunk, parts[0] if len(parts) == 1 else jnp.concatenate(parts, axis=1))
+
     for kh in range(KH):
-        base = kh * 3
-        got = tokens(base)
         lower = kh * PRE
-        keys = jnp.concatenate([pre_now[lower : lower + PRE], got[:, 0:D]], axis=0)
+        keys = jnp.concatenate([pre_now[lower : lower + PRE], rows_of("k", kh)], axis=0)
         values = jnp.concatenate(
-            [pre_now[KH * PRE + lower : KH * PRE + lower + PRE], got[:, D : 2 * D]], axis=0
+            [pre_now[KH * PRE + lower : KH * PRE + lower + PRE], rows_of("v", kh)], axis=0
         )
         keys_t = jnp.transpose(keys.astype(F32)).astype(BF16)
         key_grad = value_grad = None
-        for part in range(3):
-            if part == 0:
-                pairs = ((got[:, 2 * D : 3 * D], got[:, 3 * D :]),)
-            else:
-                got = tokens(base + part)
-                pairs = ((got[:, :D], got[:, 2 * D : 3 * D]), (got[:, D : 2 * D], got[:, 3 * D :]))
-            results = []
-            for queries, grads in pairs:
-                result, key_grad, value_grad = attend(
-                    keys, values, keys_t, queries, grads, key_grad, value_grad
-                )
-                results.append(result)
-            whole = results[0] if part == 0 else jnp.concatenate(results, axis=1)
-            back_z(kh * 4 + part, whole)
-            if kh == 1:
-                back_y(part)
-                if part > 0:
-                    back_x(part - 1)
-        own = [(key_grad[PRE:] * SCALE).astype(BF16), value_grad[PRE:].astype(BF16)]
-        back_z(kh * 4 + 3, jnp.concatenate(own, axis=1))
+        for head in range(kh * RATIO, (kh + 1) * RATIO):
+            result, key_grad, value_grad = attend(
+                keys,
+                values,
+                keys_t,
+                rows_of("q", head),
+                rows_of("c", head),
+                key_grad,
+                value_grad,
+            )
+            finish("q", head, result)
         acc[kh, 0] = key_grad[:PRE] * SCALE
         acc[kh, 1] = value_grad[:PRE]
         reduce_core(kh)
+        finish("k", kh, (key_grad[PRE:] * SCALE).astype(BF16))
+        finish("v", kh, value_grad[PRE:].astype(BF16))
         if kh == 1:
             reduce_side(0)
 
-    back_y(3)
-    back_x(2)
+    back_y(0)
+    back_y(1)
+    back_x(0)
     reduce_side(1)
-    back_y(4)
-    back_x(3)
-    reduce_end(0)
-    back_y(5)
-    back_x(4)
-    back_y(6)
-    back_x(5)
+    reduce_mate(0)
+    for chunk in range(2, BACKS):
+        back_y(chunk)
+        back_x(chunk - 1)
+        if chunk == 4:
+            reduce_mate(1)
+        if chunk == 5:
+            reduce_end(0)
     reduce_end(1)
-    back_y(7)
-    back_x(6)
     await_bytes(flag_in, t_recv.at[3])
-    overflow[...] = jnp.maximum(flag_out[...], jnp.max(flag_in[...], axis=0))
-    back_x(7)
-
-    for i in range(TP - 1):
-        await_bytes(route, t_send.at[0])
+    overflow[0] = jnp.max(jnp.maximum(flag_out[...], jnp.max(flag_in[...], axis=0))).astype(I32)
+    back_x(BACKS - 1)
+
+    await_bytes(x_table, t_send.at[0])
     await_bytes(flag_in, t_send.at[3])
     for i, ref in ((1, y_table_out), (2, z_table_out)):
         await_bytes(ref.at[:, pl.ds(0, 7 * PITCH)], t_send.at[i])
     for chunk in range(CHUNKS):
-        await_bytes(x_in.at[chunk, pl.ds(0, 3 * SEND)], x_send.at[chunk])
-        await_bytes(y_out.at[chunk, pl.ds(0, 7 * cap_y)], y_send.at[chunk])
-        await_bytes(z_out.at[chunk, pl.ds(0, 7 * cap_z)], z_send.at[chunk])
+        lanes = pl.ds(0, width(FORWARD[chunk]))
+        await_bytes(x_in.at[chunk, pl.ds(0, 3 * SEND), lanes], x_send.at[chunk])
+        await_bytes(y_out.at[chunk, pl.ds(0, 7 * cap_y), lanes], y_send.at[chunk])
+        await_bytes(z_out.at[chunk, pl.ds(0, 7 * cap_z), lanes], z_send.at[chunk])
     for chunk in range(BACKS):
-        lanes = pl.ds(0, WIDTHS[chunk % 4])
+        lanes = pl.ds(0, width(BACKWARD[chunk]))
         await_bytes(bz_out.at[chunk, pl.ds(0, 7 * cap_z), lanes], bz_send.at[chunk])
         await_bytes(by_out.at[chunk, pl.ds(0, 7 * cap_y), lanes], by_send.at[chunk])
         await_bytes(bx_out.at[chunk, pl.ds(0, 3 * SEND), lanes], bx_send.at[chunk])
         await_bytes(bx_out.at[chunk, :, lanes], bx_recv.at[chunk])
-    await_bytes(prefix, p_send.at[0])
+    await_bytes(pre_own, p_send.at[0])
     await_bytes(pre_now.at[pl.ds(0, 2 * PRE)], p_send.at[2])
     for kh in range(KH):
-        await_bytes(acc_in.at[kh], a_send.at[kh, 0])
-        await_bytes(chip.at[kh], a_send.at[kh, 1])
-        await_bytes(chip.at[kh], a_send.at[kh, 2])
-        await_bytes(chip.at[kh], a_recv.at[kh, 2])
-        await_bytes(chip.at[kh], a_recv.at[kh, 3])
+        for i in range(3):
+            await_bytes(chip.at[kh], a_send.at[kh, i])
 
 
 def whole_step(cap_y, cap_z, number, operands):
@@ -569,6 +625,7 @@
 
     dma = pltpu.SemaphoreType.DMA
     in_vmem = pl.BlockSpec(memory_space=pltpu.VMEM)
+    in_smem = pl.BlockSpec(memory_space=pltpu.SMEM)
     anywhere = pl.BlockSpec(memory_space=pl.ANY)
     return pl.pallas_call(
         functools.partial(kernel, cap_y, cap_z),
@@ -576,13 +633,14 @@
             jax.ShapeDtypeStruct((SEND, TP * KH * RATIO * D), BF16),
             jax.ShapeDtypeStruct((SEND, TP * KH * D), BF16),
             jax.ShapeDtypeStruct((SEND, TP * KH * D), BF16),
-            jax.ShapeDtypeStruct((2, KH, PRE, D), F32),
-            jax.ShapeDtypeStruct((8, PITCH), F32),
+            jax.ShapeDtypeStruct((1, PRE, 2, KH * D), F32),
+            jax.ShapeDtypeStruct((1,), I32),
         ),
-        in_specs=[anywhere] * 4 + [in_vmem] * 5,
-        out_specs=(anywhere,) * 4 + (in_vmem,),
+        in_specs=[anywhere] * 4 + [in_vmem] * 2 + [in_smem, anywhere, in_smem],
+        out_specs=(anywhere,) * 3 + (in_vmem, in_smem),
         scratch_shapes=[
-            vmem(TP - 1, 8, ROWS, dtype=I32),
+            vmem(8, SEND, dtype=F32),
+            vmem(TP - 1, 8, SEND, dtype=F32),
             vmem(8, 8 * PITCH, dtype=F32),
             vmem(8, 8 * PITCH, dtype=F32),
             vmem(8, 8 * PITCH, dtype=F32),
@@ -599,6 +657,8 @@
             vmem(BACKS, 8 * cap_y, BACK),
             vmem(BACKS, 8 * cap_y, BACK),
             vmem(BACKS, ROWS, BACK),
+            vmem(PRE, 2, KH * D),
+            vmem(2 * KH * PRE, D),
             vmem(2 * KH * PRE, D),
             vmem(2 * KH * PRE, D),
             vmem(2 * KH * PRE, D),
@@ -613,7 +673,8 @@
             vmem(KH, PRE, D, dtype=F32),
             vmem(KH, PRE, D, dtype=F32),
             vmem(KH, PRE, D, dtype=F32),
-            vmem(KH, 2, PRE, D, dtype=F32),
+            vmem(KH, PRE, D, dtype=F32),
+            vmem(KH, PRE, D, dtype=F32),
             dma((4,)),
             dma((4,)),
             dma((CHUNKS,)),
@@ -629,9 +690,9 @@
             dma((BACKS,)),
             dma((BACKS,)),
             dma((3,)),
-            dma((3,)),
+            dma((4,)),
             dma((KH, 3)),
-            dma((KH, 4)),
+            dma((KH, 3)),
         ],
         compiler_params=pltpu.CompilerParams(
             collective_id=number, has_side_effects=True, vmem_limit_bytes=60 * 2**20
@@ -639,39 +700,50 @@
     )(*operands)
 
 
+def hand_out(*refs):
+    sources, targets, sem = refs[:4], refs[4:8], refs[8]
+    copies = [
+        pltpu.make_async_copy(source, target, sem.at[i])
+        for i, (source, target) in enumerate(zip(sources, targets))
+    ]
+    for copy in copies:
+        copy.start()
+    for copy in copies:
+        copy.wait()
+
+
+def handed_out(results):
+    anywhere = pl.BlockSpec(memory_space=pl.ANY)
+    return pl.pallas_call(
+        hand_out,
+        out_shape=tuple(jax.ShapeDtypeStruct(x.shape, x.dtype) for x in results),
+        in_specs=[anywhere] * 4,
+        out_specs=(anywhere,) * 4,
+        scratch_shapes=[pltpu.SemaphoreType.DMA((4,))],
+    )(*results)
+
+
 def body(
     roll_query, roll_key, roll_value, roll_cotangent, route, arrival, lengths, prefix_kv, owner
 ):
-    tp = lax.axis_index("tp")
-    group = lax.axis_index("grp") // TP
-    line = jnp.arange(ROWS, dtype=I32) // SEND
-    routes = jnp.broadcast_to(jnp.where(line == tp, jnp.tile(route, TP), 0)[None], (8, ROWS))
-    arrivals = jnp.broadcast_to(arrival[:, None], (ROWS, D))
-    sizes = jnp.broadcast_to(
-        jnp.concatenate([lengths[0], lengths[0]])[:, None].astype(I32), (8, D)
-    )
-    held = jnp.transpose(prefix_kv[0].reshape(PRE, 2, KH, D), (1, 2, 0, 3))
-    held = held.reshape(2 * KH * PRE, D)
-    holder = jnp.broadcast_to(owner[group], (8, D))
     operands = (
         roll_query,
         roll_key,
         roll_value,
         roll_cotangent,
-        routes,
-        arrivals,
-        sizes,
-        held,
-        holder,
+        route,
+        arrival,
+        lengths,
+        prefix_kv,
+        owner,
     )
     *quick, overflow = whole_step(48, 48, 0, operands)
-    grad_query, grad_key, grad_value, grad_prefix = lax.cond(
-        overflow[0, 0] > 0.5,
+    results = lax.cond(
+        overflow[0] > 0,
         lambda: tuple(whole_step(64, 64, 1, operands)[:4]),
         lambda: tuple(quick),
     )
-    grad_prefix = jnp.transpose(grad_prefix, (2, 0, 1, 3)).reshape(1, PRE, 2, KH * D)
-    return grad_query, grad_key, grad_value, grad_prefix
+    return handed_out(results)
 
 
 def solution(mesh):

time: 137 us -> 121 us (0.88)
  local copies, waits for them, and re-layouts: 14.1 us -> 1.29 us
  Pallas kernels: 120 us -> 118 us
    unnamed x21 -> x18, local copies, waits for them, and re-layouts: 6.02 us -> 1.29 us
    pallas_call x1, Pallas kernels: 120 us -> 117 us  [whole_step(): pl.pallas_call(functools.partial(kernel, cap_y, cap_z), out_shape=(jax.Sh...]
    another operation x4 -> x0, local copies, waits for them, and re-layouts: 2.53 us -> none  [the longest x2 2.45 us: body(): held = jnp.transpose(prefix_kv[0].reshape(PRE, 2, KH, D), (1, 2, 0, 3))]
    reshape x1 -> x0, local copies, waits for them, and re-layouts: 2.17 us -> none  [body(): jnp.transpose(grad_prefix, (2, 0, 1, 3)).reshape(1, PRE, 2, KH * D)]
where the time goes in v2:
time: 121 us
  Pallas kernels  118 us (98%)
  between operations  1.5 us (1%)
  local copies, waits for them, and re-layouts  1.29 us (1%)
    pallas_call x1, Pallas kernels, whole_step(): pl.pallas_call(functools.partial(kernel, cap_y, cap_z), out_shape=(jax.Sh...  117 us

profile of v2, /device:TPU:1, one launch (start us, length us, event | category | flops | bytes accessed | tf_op | source)
XLA Modules:
  0.0 120.8 jit_solution(1875129402469063819)
XLA Ops:
  0.6 0.0 copy-start.5
  0.6 0.0 copy-start.6
  0.7 0.7 copy-done.5
  1.3 0.0 copy-done.6
  1.3 0.0 copy-start
  1.3 0.0 copy-start.1
  1.3 0.0 copy-start.2
  1.3 0.0 copy-start.3
  1.3 0.0 copy-start.4
  1.3 116.7 %shard_map.120 = (bf16[64,5120]{1,0:T(8,128)(2,1)S(1)}, bf16[64,1024]{1,0:T(8,128)(2,1)S(1)}, bf16[64,1024]{1,0:T(8,128)(2,1)S(1)}, f32[1,512,2,256]{3,2,1,0:T(2,128)S(1)}, s32[1]{0:T(128)}) custom-call(bf16[64,5120]{1,0:T(8,128)(2,1)} %query.1, bf16[64,1024]{1,0:T(8,128)(2,1)} %key.1, bf16[64,1024]{1,0:T(8,128)(2,1)} %value.1, bf16[64,5120]{1,0:T(8,128)(2,1)} %cotangent.1, ...), custom_call_target="tpu_custom_call" | custom-call | tf_op jit(solution)/shard_map/pallas_call | solution.py:630
  118.6 0.0 copy-start.7
  118.6 0.0 copy-start.8
  118.6 0.0 copy-done
  118.6 0.0 copy-done.1
  118.7 0.0 copy-done.2
  118.7 0.0 copy-done.3
  118.7 0.0 copy-done.4
  118.7 0.6 copy-done.7
  119.3 0.0 copy-done.8
  119.3 1.3 %shard_map.121 = (bf16[64,5120]{1,0:T(8,128)(2,1)}, bf16[64,1024]{1,0:T(8,128)(2,1)}, bf16[64,1024]{1,0:T(8,128)(2,1)}, f32[1,512,2,256]{3,2,1,0:T(2,128)}) custom-call(bf16[64,5120]{1,0:T(8,128)(2,1)S(1)} %get-tuple-element.57.refs_0_, bf16[64,1024]{1,0:T(8,128)(2,1)S(1)} %get-tuple-element.58.refs_1_, bf16[64,1024]{1,0:T(8,128)(2,1)S(1)} %get-tuple-element.59.refs_2_, ...), custom_call_target="tpu_custom_call" | custom-call | tf_op jit(solution)/shard_map/pallas_call | solution.py:717
  (1 shorter events, 0.0 us)
Async XLA Ops:
  0.6 0.7 copy-start.5
  0.6 0.7 copy-start.6
  1.3 117.3 %copy-start = (bf16[64,5120]{1,0:T(8,128)(2,1)S(1)}, bf16[64,5120]{1,0:T(8,128)(2,1)}, u32[]{:S(2)}) copy-start(bf16[64,5120]{1,0:T(8,128)(2,1)} %query.1) | copy-start | bytes 1966084
  1.3 117.3 %copy-start.1 = (bf16[64,5120]{1,0:T(8,128)(2,1)S(1)}, bf16[64,5120]{1,0:T(8,128)(2,1)}, u32[]{:S(2)}) copy-start(bf16[64,5120]{1,0:T(8,128)(2,1)} %cotangent.1) | copy-start | bytes 1966084
  1.3 117.3 %copy-start.2 = (bf16[1,512,2,256]{3,2,1,0:T(2,128)(2,1)S(1)}, bf16[1,512,2,256]{3,2,1,0:T(2,128)(2,1)}, u32[]{:S(2)}) copy-start(bf16[1,512,2,256]{3,2,1,0:T(2,128)(2,1)} %prefix.1) | copy-start | bytes 1572868
  1.3 117.3 %copy-start.3 = (bf16[64,1024]{1,0:T(8,128)(2,1)S(1)}, bf16[64,1024]{1,0:T(8,128)(2,1)}, u32[]{:S(2)}) copy-start(bf16[64,1024]{1,0:T(8,128)(2,1)} %key.1) | copy-start | bytes 393220
  1.3 117.3 %copy-start.4 = (bf16[64,1024]{1,0:T(8,128)(2,1)S(1)}, bf16[64,1024]{1,0:T(8,128)(2,1)}, u32[]{:S(2)}) copy-start(bf16[64,1024]{1,0:T(8,128)(2,1)} %value.1) | copy-start | bytes 393220
  118.6 0.7 copy-start.7
  118.6 0.7 copy-start.8

commit v3 on v2

--- a/solution.py
+++ b/solution.py
@@ -18,8 +18,9 @@
 SEND = 64
 PRE = 512
 FORWARD = (
-    (("k", 0, 1), ("v", 0, 1)),
-    (("q", 0, 1), ("c", 0, 1)),
+    (("k", 0, 1),),
+    (("v", 0, 1), ("q", 0, 1)),
+    (("c", 0, 1),),
     (("q", 1, 2), ("c", 1, 2)),
     (("q", 3, 2), ("c", 3, 2)),
     (("k", 1, 1), ("v", 1, 1), ("q", 5, 1), ("c", 5, 1)),
@@ -36,7 +37,8 @@
     (("q", 6, 2),),
     (("q", 8, 1),),
     (("q", 9, 1),),
-    (("k", 1, 1), ("v", 1, 1)),
+    (("k", 1, 1),),
+    (("v", 1, 1),),
 )
 CHUNKS = len(FORWARD)
 BACKS = len(BACKWARD)
@@ -81,10 +83,21 @@
     return lax.dot_general(a, b, (((1,), (1,)), ((), ())), preferred_element_type=F32)
 
 
-def place(kind, valid, lanes, limit):
+def earlier(lanes):
+    return hot(iota((lanes, lanes), 0) < iota((lanes, lanes), 1))
+
+
+def picking(limit):
+    lane = iota((8 * PITCH, 8 * limit), 1)
+    target = lane
+    for i in range(1, 8):
+        target = target + jnp.where(lane >= i * limit, PITCH - limit, 0)
+    return hot(iota((8 * PITCH, 8 * limit), 0) == target)
+
+
+def place(kind, valid, lanes, limit, before):
     classes = iota((8, lanes), 0)
     member = (kind == classes) & valid
-    before = hot(iota((lanes, lanes), 0) < iota((lanes, lanes), 1))
     count = dot(hot(member), before)
     rank = jnp.sum(jnp.where(member, count, 0.0), axis=0, keepdims=True).astype(I32)
     kind, valid = kind[0:1], valid[0:1]
@@ -106,13 +119,7 @@
     return jnp.max(table[2:3], axis=1, keepdims=True)
 
 
-def compacted(table, limit, column=False):
-    lanes = 8 * limit
-    lane = iota((8 * PITCH, lanes), 1)
-    target = lane
-    for i in range(1, 8):
-        target = target + jnp.where(lane >= i * limit, PITCH - limit, 0)
-    pick = hot(iota((8 * PITCH, lanes), 0) == target)
+def compacted(table, pick, column=False):
     if column:
         parts = lax.dot_general(
             pick, table.astype(BF16), (((0,), (1,)), ((), ())), preferred_element_type=F32
@@ -175,6 +182,9 @@
     from_z,
     from_rows,
     mask,
+    before_y,
+    before_z,
+    pick_y,
     acc,
     acc_in,
     chip,
@@ -256,6 +266,9 @@
         pl.semaphore_signal(entry, inc=1, device_id=at_y(k), device_id_type=MESH)
     for k in range(1, PLANE):
         pl.semaphore_signal(entry, inc=1, device_id=at_z(k), device_id_type=MESH)
+    before_y[...] = earlier(ROWS)
+    before_z[...] = earlier(8 * cap_y)
+    pick_y[...] = picking(cap_y)
     pl.semaphore_wait(entry, TP - 1 + 2 * (PLANE - 1))
 
     x_table_out[...] = jnp.broadcast_to(route[...].reshape(1, SEND), (8, SEND)).astype(F32)
@@ -305,7 +318,7 @@
     line = iota((8, ROWS), 1) // SEND
     number = grp * (2 * TP) + line * 2 + (routes & 1)
     code = ((trainer >> 3) * 512 + number + 1)[0:1]
-    slot, table, over = place(trainer & 7, trainer >= 0, ROWS, cap_y)
+    slot, table, over = place(trainer & 7, trainer >= 0, ROWS, cap_y, before_y[...])
     to_y[...] = hot(iota((8 * cap_y, ROWS), 0) == slot)
     y_table_out[...] = tabulate(code, table, over, ROWS)
     for k in range(1, PLANE):
@@ -363,11 +376,12 @@
     y_stage(1)
 
     await_bytes(y_table_in, t_recv.at[1])
-    code = compacted(y_table_in[...], cap_y)
+    code = compacted(y_table_in[...], pick_y[...])
     lanes = 8 * cap_y
     code8 = jnp.broadcast_to(code, (8, lanes))
-    slot, table, over = place((code8 - 1) >> 9, code8 > 0, lanes, cap_z)
+    slot, table, over = place((code8 - 1) >> 9, code8 > 0, lanes, cap_z, before_z[...])
     to_z[...] = hot(iota((8 * cap_z, lanes), 0) == slot)
+    z_stage(0)
     over = jnp.maximum(over, flagged(y_table_in[...]))
     z_table_out[...] = tabulate(((code - 1) & 511) + 1, table, over, lanes)
     for k in range(1, PLANE):
@@ -381,8 +395,6 @@
     local(
         z_table_out.at[:, block(plane, PITCH)], z_table_in.at[:, block(plane, PITCH)], t_recv.at[2]
     )
-
-    z_stage(0)
 
     hold = owner[grp // TP]
 
@@ -435,7 +447,7 @@
     flag_out[...] = jnp.broadcast_to(flagged(z_table_in[...]), (8, PITCH))
     for k in range(1, PLANE):
         remote(flag_out, flag_in.at[k - 1], t_send.at[3], t_recv.at[3], at_y(k))
-    code = compacted(z_table_in[...], cap_z, column=True) - 1
+    code = compacted(z_table_in[...], picking(cap_z), column=True) - 1
     rows = hot(code == arrival[...].reshape(1, ROWS))
     from_rows[...] = rows
     to_rows[...] = turned(rows)
@@ -580,22 +592,20 @@
         if kh == 1:
             reduce_side(0)
 
-    back_y(0)
-    back_y(1)
-    back_x(0)
-    reduce_side(1)
-    reduce_mate(0)
-    for chunk in range(2, BACKS):
-        back_y(chunk)
-        back_x(chunk - 1)
-        if chunk == 4:
+    for step in range(BACKS + 2):
+        if step < BACKS:
+            back_y(step)
+        if step >= 2:
+            back_x(step - 2)
+        if step == 2:
+            reduce_side(1)
+            reduce_mate(0)
+        if step == 6:
             reduce_mate(1)
-        if chunk == 5:
             reduce_end(0)
     reduce_end(1)
     await_bytes(flag_in, t_recv.at[3])
     overflow[0] = jnp.max(jnp.maximum(flag_out[...], jnp.max(flag_in[...], axis=0))).astype(I32)
-    back_x(BACKS - 1)
 
     await_bytes(x_table, t_send.at[0])
     await_bytes(flag_in, t_send.at[3])
@@ -626,6 +636,7 @@
     dma = pltpu.SemaphoreType.DMA
     in_vmem = pl.BlockSpec(memory_space=pltpu.VMEM)
     in_smem = pl.BlockSpec(memory_space=pltpu.SMEM)
+    in_hbm = pl.BlockSpec(memory_space=pltpu.HBM)
     anywhere = pl.BlockSpec(memory_space=pl.ANY)
     return pl.pallas_call(
         functools.partial(kernel, cap_y, cap_z),
@@ -636,7 +647,7 @@
             jax.ShapeDtypeStruct((1, PRE, 2, KH * D), F32),
             jax.ShapeDtypeStruct((1,), I32),
         ),
-        in_specs=[anywhere] * 4 + [in_vmem] * 2 + [in_smem, anywhere, in_smem],
+        in_specs=[in_hbm] * 4 + [in_vmem] * 2 + [in_smem, anywhere, in_smem],
         out_specs=(anywhere,) * 3 + (in_vmem, in_smem),
         scratch_shapes=[
             vmem(8, SEND, dtype=F32),
@@ -669,6 +680,9 @@
             vmem(8 * cap_y, 8 * cap_z),
             vmem(8 * cap_z, ROWS),
             vmem(ROWS, ROWS, dtype=F32),
+            vmem(ROWS, ROWS),
+            vmem(8 * cap_y, 8 * cap_y),
+            vmem(8 * PITCH, 8 * cap_y),
             vmem(KH, 2, PRE, D, dtype=F32),
             vmem(KH, PRE, D, dtype=F32),
             vmem(KH, PRE, D, dtype=F32),

time: 121 us -> 116 us (0.959)
  Pallas kernels: 118 us -> 113 us
    pallas_call x1, Pallas kernels: 117 us -> 112 us  [whole_step(): pl.pallas_call(functools.partial(kernel, cap_y, cap_z), out_shape=(jax.Sh...]
where the time goes in v3:
time: 116 us
  Pallas kernels  113 us (97%)
  between operations  1.52 us (1%)
  local copies, waits for them, and re-layouts  1.29 us (1%)
    pallas_call x1, Pallas kernels, whole_step(): pl.pallas_call(functools.partial(kernel, cap_y, cap_z), out_shape=(jax.Sh...  112 us

profile of v3, /device:TPU:1, one launch (start us, length us, event | category | flops | bytes accessed | tf_op | source)
XLA Modules:
  0.0 115.8 jit_solution(2995744619228007437)
XLA Ops:
  0.6 0.0 copy-start.5
  0.6 0.0 copy-start.6
  0.7 0.7 copy-done.5
  1.3 0.0 copy-done.6
  1.3 0.0 copy-start
  1.3 0.0 copy-start.1
  1.3 0.0 copy-start.2
  1.3 0.0 copy-start.3
  1.3 0.0 copy-start.4
  1.3 111.7 %shard_map.120 = (bf16[64,5120]{1,0:T(8,128)(2,1)S(1)}, bf16[64,1024]{1,0:T(8,128)(2,1)S(1)}, bf16[64,1024]{1,0:T(8,128)(2,1)S(1)}, f32[1,512,2,256]{3,2,1,0:T(2,128)S(1)}, s32[1]{0:T(128)}) custom-call(bf16[64,5120]{1,0:T(8,128)(2,1)} %query.1, bf16[64,1024]{1,0:T(8,128)(2,1)} %key.1, bf16[64,1024]{1,0:T(8,128)(2,1)} %value.1, bf16[64,5120]{1,0:T(8,128)(2,1)} %cotangent.1, ...), custom_call_target="tpu_custom_call" | custom-call | tf_op jit(solution)/shard_map/pallas_call | solution.py:641
  113.6 0.0 copy-start.7
  113.6 0.0 copy-start.8
  113.7 0.0 copy-done
  113.7 0.0 copy-done.1
  113.7 0.0 copy-done.2
  113.7 0.0 copy-done.3
  113.7 0.0 copy-done.4
  113.7 0.6 copy-done.7
  114.3 0.0 copy-done.8
  114.3 1.3 %shard_map.121 = (bf16[64,5120]{1,0:T(8,128)(2,1)}, bf16[64,1024]{1,0:T(8,128)(2,1)}, bf16[64,1024]{1,0:T(8,128)(2,1)}, f32[1,512,2,256]{3,2,1,0:T(2,128)}) custom-call(bf16[64,5120]{1,0:T(8,128)(2,1)S(1)} %get-tuple-element.57.refs_0_, bf16[64,1024]{1,0:T(8,128)(2,1)S(1)} %get-tuple-element.58.refs_1_, bf16[64,1024]{1,0:T(8,128)(2,1)S(1)} %get-tuple-element.59.refs_2_, ...), custom_call_target="tpu_custom_call" | custom-call | tf_op jit(solution)/shard_map/pallas_call | solution.py:731
  (1 shorter events, 0.0 us)
Async XLA Ops:
  0.6 0.7 copy-start.5
  0.6 0.7 copy-start.6
  1.3 112.3 %copy-start = (bf16[64,5120]{1,0:T(8,128)(2,1)S(1)}, bf16[64,5120]{1,0:T(8,128)(2,1)}, u32[]{:S(2)}) copy-start(bf16[64,5120]{1,0:T(8,128)(2,1)} %query.1) | copy-start | bytes 1966084
  1.3 112.4 %copy-start.1 = (bf16[64,5120]{1,0:T(8,128)(2,1)S(1)}, bf16[64,5120]{1,0:T(8,128)(2,1)}, u32[]{:S(2)}) copy-start(bf16[64,5120]{1,0:T(8,128)(2,1)} %cotangent.1) | copy-start | bytes 1966084
  1.3 112.4 %copy-start.2 = (bf16[1,512,2,256]{3,2,1,0:T(2,128)(2,1)S(1)}, bf16[1,512,2,256]{3,2,1,0:T(2,128)(2,1)}, u32[]{:S(2)}) copy-start(bf16[1,512,2,256]{3,2,1,0:T(2,128)(2,1)} %prefix.1) | copy-start | bytes 1572868
  1.3 112.4 %copy-start.3 = (bf16[64,1024]{1,0:T(8,128)(2,1)S(1)}, bf16[64,1024]{1,0:T(8,128)(2,1)}, u32[]{:S(2)}) copy-start(bf16[64,1024]{1,0:T(8,128)(2,1)} %key.1) | copy-start | bytes 393220
  1.3 112.4 %copy-start.4 = (bf16[64,1024]{1,0:T(8,128)(2,1)S(1)}, bf16[64,1024]{1,0:T(8,128)(2,1)}, u32[]{:S(2)}) copy-start(bf16[64,1024]{1,0:T(8,128)(2,1)} %value.1) | copy-start | bytes 393220
  113.6 0.7 copy-start.7
  113.6 0.7 copy-start.8

commit v4 on v3

--- a/solution.py
+++ b/solution.py
@@ -188,6 +188,7 @@
     acc,
     acc_in,
     chip,
+    chip_out,
     chip_in,
     total,
     total_in,
@@ -512,11 +513,12 @@
     def reduce_side(kh):
         await_bytes(acc_in.at[kh], a_recv.at[kh, 0])
         chip[kh] = acc[kh, core] + acc_in[kh]
-        remote(chip.at[kh], chip_in.at[kh], a_send.at[kh, 1], a_recv.at[kh, 1], (across, tp))
+        chip_out[kh] = chip[kh].astype(BF16)
+        remote(chip_out.at[kh], chip_in.at[kh], a_send.at[kh, 1], a_recv.at[kh, 1], (across, tp))
 
     def reduce_mate(kh):
         await_bytes(chip_in.at[kh], a_recv.at[kh, 1])
-        total[kh] = chip[kh] + chip_in[kh]
+        total[kh] = chip[kh] + chip_in[kh].astype(F32)
         remote(total.at[kh], total_in.at[kh], a_send.at[kh, 2], a_recv.at[kh, 2], (mate, tp))
 
     def reduce_end(kh):
@@ -625,8 +627,9 @@
     await_bytes(pre_own, p_send.at[0])
     await_bytes(pre_now.at[pl.ds(0, 2 * PRE)], p_send.at[2])
     for kh in range(KH):
-        for i in range(3):
-            await_bytes(chip.at[kh], a_send.at[kh, i])
+        await_bytes(chip.at[kh], a_send.at[kh, 0])
+        await_bytes(chip_out.at[kh], a_send.at[kh, 1])
+        await_bytes(chip.at[kh], a_send.at[kh, 2])
 
 
 def whole_step(cap_y, cap_z, number, operands):
@@ -686,7 +689,8 @@
             vmem(KH, 2, PRE, D, dtype=F32),
             vmem(KH, PRE, D, dtype=F32),
             vmem(KH, PRE, D, dtype=F32),
-            vmem(KH, PRE, D, dtype=F32),
+            vmem(KH, PRE, D),
+            vmem(KH, PRE, D),
             vmem(KH, PRE, D, dtype=F32),
             vmem(KH, PRE, D, dtype=F32),
             dma((4,)),

time: 116 us -> 116 us (level)
  no operation moved by 1% of the time
where the time goes in v4:
time: 116 us
  Pallas kernels  113 us (97%)
  between operations  1.52 us (1%)
  local copies, waits for them, and re-layouts  1.29 us (1%)
    pallas_call x1, Pallas kernels, whole_step(): pl.pallas_call(functools.partial(kernel, cap_y, cap_z), out_shape=(jax.Sh...  112 us

profile of v4, /device:TPU:1, one launch (start us, length us, event | category | flops | bytes accessed | tf_op | source)
XLA Modules:
  0.0 115.8 jit_solution(17437244052089697107)
XLA Ops:
  0.6 0.0 copy-start.5
  0.6 0.0 copy-start.6
  0.7 0.7 copy-done.5
  1.3 0.0 copy-done.6
  1.3 0.0 copy-start
  1.3 0.0 copy-start.1
  1.3 0.0 copy-start.2
  1.3 0.0 copy-start.3
  1.3 0.0 copy-start.4
  1.3 111.7 %shard_map.120 = (bf16[64,5120]{1,0:T(8,128)(2,1)S(1)}, bf16[64,1024]{1,0:T(8,128)(2,1)S(1)}, bf16[64,1024]{1,0:T(8,128)(2,1)S(1)}, f32[1,512,2,256]{3,2,1,0:T(2,128)S(1)}, s32[1]{0:T(128)}) custom-call(bf16[64,5120]{1,0:T(8,128)(2,1)} %query.1, bf16[64,1024]{1,0:T(8,128)(2,1)} %key.1, bf16[64,1024]{1,0:T(8,128)(2,1)} %value.1, bf16[64,5120]{1,0:T(8,128)(2,1)} %cotangent.1, ...), custom_call_target="tpu_custom_call" | custom-call | tf_op jit(solution)/shard_map/pallas_call | solution.py:644
  113.6 0.0 copy-start.7
  113.6 0.0 copy-start.8
  113.7 0.0 copy-done
  113.7 0.0 copy-done.1
  113.7 0.0 copy-done.2
  113.7 0.0 copy-done.3
  113.7 0.0 copy-done.4
  113.7 0.6 copy-done.7
  114.3 0.0 copy-done.8
  114.3 1.3 %shard_map.121 = (bf16[64,5120]{1,0:T(8,128)(2,1)}, bf16[64,1024]{1,0:T(8,128)(2,1)}, bf16[64,1024]{1,0:T(8,128)(2,1)}, f32[1,512,2,256]{3,2,1,0:T(2,128)}) custom-call(bf16[64,5120]{1,0:T(8,128)(2,1)S(1)} %get-tuple-element.57.refs_0_, bf16[64,1024]{1,0:T(8,128)(2,1)S(1)} %get-tuple-element.58.refs_1_, bf16[64,1024]{1,0:T(8,128)(2,1)S(1)} %get-tuple-element.59.refs_2_, ...), custom_call_target="tpu_custom_call" | custom-call | tf_op jit(solution)/shard_map/pallas_call | solution.py:735
  (1 shorter events, 0.0 us)
Async XLA Ops:
  0.6 0.7 copy-start.5
  0.6 0.7 copy-start.6
  1.3 112.3 %copy-start = (bf16[64,5120]{1,0:T(8,128)(2,1)S(1)}, bf16[64,5120]{1,0:T(8,128)(2,1)}, u32[]{:S(2)}) copy-start(bf16[64,5120]{1,0:T(8,128)(2,1)} %query.1) | copy-start | bytes 1966084
  1.3 112.4 %copy-start.1 = (bf16[64,5120]{1,0:T(8,128)(2,1)S(1)}, bf16[64,5120]{1,0:T(8,128)(2,1)}, u32[]{:S(2)}) copy-start(bf16[64,5120]{1,0:T(8,128)(2,1)} %cotangent.1) | copy-start | bytes 1966084
  1.3 112.4 %copy-start.2 = (bf16[1,512,2,256]{3,2,1,0:T(2,128)(2,1)S(1)}, bf16[1,512,2,256]{3,2,1,0:T(2,128)(2,1)}, u32[]{:S(2)}) copy-start(bf16[1,512,2,256]{3,2,1,0:T(2,128)(2,1)} %prefix.1) | copy-start | bytes 1572868
  1.3 112.4 %copy-start.3 = (bf16[64,1024]{1,0:T(8,128)(2,1)S(1)}, bf16[64,1024]{1,0:T(8,128)(2,1)}, u32[]{:S(2)}) copy-start(bf16[64,1024]{1,0:T(8,128)(2,1)} %key.1) | copy-start | bytes 393220
  1.3 112.4 %copy-start.4 = (bf16[64,1024]{1,0:T(8,128)(2,1)S(1)}, bf16[64,1024]{1,0:T(8,128)(2,1)}, u32[]{:S(2)}) copy-start(bf16[64,1024]{1,0:T(8,128)(2,1)} %value.1) | copy-start | bytes 393220
  113.6 0.7 copy-start.7
  113.6 0.7 copy-start.8
